TPU v7x, 128 devices: a whole 4x4x4 slice. The times are simulated.
128 devices in a mesh: dp: 4 (over y), seq: 4 (over x), expert: 8 (over z, core).
Axes of the slice: x: 4, y: 4, z: 4, core: 2. Of those that a mesh axis runs over, the one named last changes fastest.
Arguments:
- queries: bfloat16 [32, 512, 2048], P(('dp', 'expert'), 'seq'), may hold values from -135 to 135
- keys: bfloat16 [32, 512, 2048], P(('dp', 'expert'), 'seq'), may hold values from -5 to 5
- values: bfloat16 [32, 512, 2048], P(('dp', 'expert'), 'seq'), may hold values from -6 to 6
- resid: bfloat16 [32, 512, 2048], P(('dp', 'expert'), 'seq'), may hold values from -20 to 20
- cotangent: bfloat16 [32, 512, 2048], P(('dp', 'expert'), 'seq'), may hold values from -0.3125 to 0.3125
- zone_ids: int32 [32, 512, 1], P(('dp', 'expert'), 'seq'), may hold values from 0 to 31; in each aligned block of 128 rows (0 to 127, 128 to 255, ..., all dimensions but the last counted through in order) at most 10 rows name the same one
- norm_gain: float32 [2048], replicated, may hold values from 0.1 to 1.9
- w_in: bfloat16 [32, 2048, 4096], P(('seq', 'expert'), None, 'dp'), may hold values from -0.125 to 0.125
- w_out: bfloat16 [32, 4096, 2048], P(('seq', 'expert'), 'dp'), may hold values from -0.09375 to 0.09375
Outputs:
- layer_out: bfloat16 [32, 512, 2048], P(('dp', 'expert'), 'seq')
- grad_w_in: bfloat16 [32, 2048, 4096], P(('seq', 'expert'), None, 'dp')
- grad_w_out: bfloat16 [32, 4096, 2048], P(('seq', 'expert'), 'dp')
Inputs may be any that keep to these rules, and one draw needn't show every extreme that they name: `zone_ids`: among the tokens of one device at most 10 name the same expert, and that count is reached.
All inputs are finite; a program needn't handle non-finite values.
Results may differ from a plain program's by a relative error of at most 0.0085.
Values may be sent and summed in bfloat16 or wider, within the bound.
No kernel may reach another device: no remote copies, remote signals or barrier semaphores. Data moves between devices by JAX's collectives and lax.ppermute only.
A program may use at most 128 MiB of HBM per device.

v0:
```python
import math

import jax
import jax.numpy as jnp
from jax import lax
from jax.sharding import PartitionSpec as P

HEADS = 16


epsilon = 1e-05


def shards(queries, keys, values, resid, cotangent, zone_ids, norm_gain, w_in, w_out):
    local_rows = queries.shape[1]
    model_width = queries.shape[2]
    head_dim = model_width // HEADS
    score_scale = 1.0 / math.sqrt(head_dim)
    q_heads = queries[0].reshape(local_rows, HEADS, head_dim)
    peak_now = jnp.full((HEADS, local_rows), -jnp.inf, jnp.float32)
    totals = jnp.zeros((HEADS, local_rows), jnp.float32)
    accum = jnp.zeros((HEADS, local_rows, head_dim), jnp.float32)
    key_block = lax.all_gather(keys, "seq", axis=1, tiled=True)
    value_block = lax.all_gather(values, "seq", axis=1, tiled=True)
    count = key_block.shape[1]
    k_heads = key_block[0].reshape(count, HEADS, head_dim)
    v_heads = value_block[0].reshape(count, HEADS, head_dim)
    scores = (
        jnp.einsum("shd,thd->hst", q_heads, k_heads, preferred_element_type=jnp.float32)
        * score_scale
    )
    newest = jnp.max(scores, axis=-1)
    factor = jnp.exp(peak_now - newest)
    weights = jnp.exp(scores - newest[..., None])
    totals = totals * factor + jnp.sum(weights, axis=-1)
    accum = accum * factor[..., None] + jnp.einsum(
        "hst,thd->hsd", weights.astype(jnp.bfloat16), v_heads, preferred_element_type=jnp.float32
    )
    peak_now, totals, accum = (newest, totals, accum)
    attended = (accum / totals[..., None]).transpose(1, 0, 2).reshape(local_rows, model_width)
    mixed = resid[0].astype(jnp.float32) + attended
    mean_sq = jnp.mean(mixed * mixed, axis=-1, keepdims=True)
    normed = (mixed * lax.rsqrt(mean_sq + epsilon) * norm_gain).astype(jnp.bfloat16)
    owners = lax.axis_size("seq") * lax.axis_size("expert")
    groups = lax.axis_size("dp")
    capacity = 2 * local_rows // owners + 2
    zone_of = zone_ids[0, :, 0]
    expert_hot = (zone_of[:, None] == jnp.arange(owners, dtype=jnp.int32)[None, :]).astype(
        jnp.int32
    )
    ranking = jnp.cumsum(expert_hot, axis=0) - 1
    slot_index = jnp.sum(ranking * expert_hot, axis=1)
    target = zone_of * capacity + slot_index
    placing = (target[None, :] == jnp.arange(owners * capacity, dtype=jnp.int32)[:, None]).astype(
        jnp.bfloat16
    )
    send_x = jnp.dot(placing, normed, preferred_element_type=jnp.float32).astype(jnp.bfloat16)
    send_g = jnp.dot(placing, cotangent[0], preferred_element_type=jnp.float32).astype(jnp.bfloat16)
    send_x = send_x.reshape(owners, capacity, model_width)
    send_g = send_g.reshape(owners, capacity, model_width)
    wide_x = jnp.broadcast_to(send_x[None], (groups, owners, capacity, model_width)).reshape(
        groups * owners, capacity, model_width
    )
    wide_g = jnp.broadcast_to(send_g[None], (groups, owners, capacity, model_width)).reshape(
        groups * owners, capacity, model_width
    )
    arrived_x, arrived_g = (
        lax.all_to_all(wide_x, ("dp", "seq", "expert"), split_axis=0, concat_axis=0, tiled=True),
        lax.all_to_all(wide_g, ("dp", "seq", "expert"), split_axis=0, concat_axis=0, tiled=True),
    )
    slot_count = groups * owners * capacity
    inputs = arrived_x.reshape(slot_count, model_width)
    grads_in = arrived_g.reshape(slot_count, model_width)
    w_first = w_in[0]
    w_second = w_out[0]
    pre_act = jnp.dot(inputs, w_first, preferred_element_type=jnp.float32)
    activated, pull_back = jax.vjp(jax.nn.gelu, pre_act)
    hidden = activated.astype(jnp.bfloat16)
    back_proj = lax.dot_general(
        grads_in, w_second, (((1,), (1,)), ((), ())), preferred_element_type=jnp.float32
    )
    d_pre = pull_back(back_proj)[0].astype(jnp.bfloat16)
    grad_first = lax.dot_general(
        inputs, d_pre, (((0,), (0,)), ((), ())), preferred_element_type=jnp.float32
    ).astype(jnp.bfloat16)
    grad_second = lax.dot_general(
        hidden, grads_in, (((0,), (0,)), ((), ())), preferred_element_type=jnp.float32
    ).astype(jnp.bfloat16)
    summed = lax.psum_scatter(
        jnp.dot(hidden, w_second, preferred_element_type=jnp.float32).astype(jnp.bfloat16),
        "dp",
        scatter_dimension=0,
        tiled=True,
    )
    returned = lax.all_to_all(
        summed.reshape(owners, capacity, model_width),
        ("seq", "expert"),
        split_axis=0,
        concat_axis=0,
        tiled=True,
    )
    expert_rows = lax.dot_general(
        placing,
        returned.reshape(owners * capacity, model_width),
        (((0,), (0,)), ((), ())),
        preferred_element_type=jnp.float32,
    )
    layer_out = (mixed + expert_rows).astype(jnp.bfloat16)[None]
    return (layer_out, grad_first[None], grad_second[None])


def solution(mesh):
    placed = (
        P(("dp", "expert"), "seq", None),
        P(("dp", "expert"), "seq", None),
        P(("dp", "expert"), "seq", None),
        P(("dp", "expert"), "seq", None),
        P(("dp", "expert"), "seq", None),
        P(("dp", "expert"), "seq", None),
        P(),
        P(("seq", "expert"), None, "dp"),
        P(("seq", "expert"), "dp", None),
    )
    return jax.shard_map(
        shards,
        mesh=mesh,
        in_specs=placed,
        out_specs=(
            P(("dp", "expert"), "seq", None),
            P(("seq", "expert"), None, "dp"),
            P(("seq", "expert"), "dp", None),
        ),
        check_vma=False,
    )
```

profile of v0, /device:TPU:1, one launch (start us, length us, event | category | flops | bytes accessed | tf_op | source)
XLA Modules:
  0.0 437.0 jit_solution(5557800501680236186)
XLA Ops:
  7.2 2.1 copy.16
  9.4 0.7 all-gather.5.cloned.1.call-update
  10.1 1.1 copy.23
  11.3 2.2 copy.21
  13.5 0.7 fusion.42
  14.4 0.8 select_reduce_fusion
  15.9 31.2 %all-gather.3.cloned.1.call-done = bf16[1,512,2048]{1,2,0:T(8,128)(2,1)} async-done(((bf16[1,128,2048]{1,2,0:T(8,128)(2,1)}), bf16[1,512,2048]{1,2,0:T(8,128)(2,1)}) %all-gather.3.cloned.1.call-update) | async-done | bytes 2097168 | tf_op jit(solution)/shard_map/all_gather | solution.py:23
  47.1 2.4 multiply_reduce_fusion
  49.5 2.0 copy-done.2
  51.5 1.3 fusion.14
  52.8 28.6 %all-gather.5.cloned.1.call-done = bf16[1,512,2048]{2,1,0:T(8,128)(2,1)} async-done(((bf16[1,128,2048]{2,1,0:T(8,128)(2,1)}), bf16[1,512,2048]{2,1,0:T(8,128)(2,1)}) %all-gather.5.cloned.1.call-update) | async-done | bytes 2097168 | tf_op jit(solution)/shard_map/all_gather | solution.py:24
  81.4 2.9 copy.19
  84.3 4.7 %multiply_reduce_fusion.1 = (f32[128]{0:T(128)S(1)}, f32[128,16,128]{0,2,1:T(8,128)}) fusion(f32[128,16,128]{0,2,1:T(8,128)} %bitcast.63, f32[128,16]{0,1:T(8,128)S(1)} %bitcast_add_fusion.2, bf16[512,16,128]{0,2,1:T(8,128)(2,1)S(1)} %bitcast.60, f32[16,128,512]{2,1,0:T(8,128)} %copy-done.2, f32[16,128]{1,0:T(8,128)S(1)} %get-tuple-element.3, ...), kind=kOutput, calls=%fused_computation.34 | convolution fusion | flops 272891776 | bytes 8413696 | tf_op jit(solution)/shard_map/hst,thd->hsd/dot_general | solution.py:36
  89.0 1.6 copy.20
  91.2 1.5 broadcast_in_dim.40
  92.8 2.6 broadcast_in_dim.41
  95.4 106.8 %all_to_all.15 = bf16[128,10,2048]{2,1,0:T(8,128)(2,1)} all-to-all(bf16[128,10,2048]{2,1,0:T(8,128)(2,1)S(1)} %bitcast.58), channel_id=1, replica_groups=mesh['dp'=4,'seq'=4,'expert'=8] {'dp','seq','expert'}, dimensions={0} | all-to-all | bytes 10485760 | tf_op jit(solution)/shard_map/all_to_all | solution.py:68
  202.2 9.8 %reshape.65 = bf16[1280,2048]{1,0:T(8,128)(2,1)} reshape(bf16[128,10,2048]{2,1,0:T(8,128)(2,1)} %all_to_all.15) | data formatting | bytes 10485760 | tf_op jit(solution)/shard_map/reshape | solution.py:72
  212.0 8.9 %fusion.12 = f32[1280,1024]{1,0:T(8,128)S(1)} fusion(bf16[1280,2048]{1,0:T(8,128)(2,1)} %reshape.65, bf16[1,2048,1024]{2,1,0:T(8,128)(2,1)} %param.16), kind=kOutput, calls=%fused_computation.14 | convolution fusion | flops 5368709120 | bytes 14680064 | tf_op jit(solution)/shard_map/dot_general | solution.py:76
  220.9 2.4 copy-done.6
  223.3 7.7 %convolution_convert_fusion = bf16[1280,2048]{1,0:T(8,128)(2,1)} fusion(bf16[1,1024,2048]{2,1,0:T(8,128)(2,1)S(1)} %copy-done.5, f32[1280,1024]{1,0:T(8,128)S(1)} %fusion.12), kind=kOutput, calls=%fused_computation | convolution fusion | flops 5383127040 | bytes 14680064 | tf_op jit(solution)/shard_map/dot_general | solution.py:90
  231.5 1.5 broadcast_in_dim.43
  233.1 2.6 broadcast_in_dim.44
  235.7 122.4 %all_to_all.16 = bf16[128,10,2048]{2,1,0:T(8,128)(2,1)} all-to-all(bf16[128,10,2048]{2,1,0:T(8,128)(2,1)S(1)} %bitcast.59), channel_id=1, replica_groups=mesh['dp'=4,'seq'=4,'expert'=8] {'dp','seq','expert'}, dimensions={0} | all-to-all | bytes 10485760 | tf_op jit(solution)/shard_map/all_to_all | solution.py:69
  358.1 9.9 %reshape.69 = bf16[1280,2048]{1,0:T(8,128)(2,1)} reshape(bf16[128,10,2048]{2,1,0:T(8,128)(2,1)} %all_to_all.16) | data formatting | bytes 10485760 | tf_op jit(solution)/shard_map/reshape | solution.py:73
  368.0 20.1 %convert_bitcast_fusion.1 = bf16[1,2048,1024]{2,1,0:T(8,128)(2,1)} fusion(bf16[1280,2048]{1,0:T(8,128)(2,1)} %reshape.65, f32[1280,1024]{1,0:T(8,128)} %copy-done.6, bf16[1280,2048]{1,0:T(8,128)(2,1)} %reshape.69, bf16[1,1024,2048]{2,1,0:T(8,128)(2,1)} %param.17), kind=kOutput, calls=%fused_computation.17 | convolution fusion | flops 10765729792 | bytes 24117248 | tf_op jit(solution)/shard_map/dot_general | solution.py:83
  388.1 3.4 reshape.66
  391.5 6.9 %all-to-all-start.1 = ((bf16[32,10,2048]{2,1,0:T(8,128)(2,1)}), bf16[32,10,2048]{2,1,0:T(8,128)(2,1)}, u32[]{:S(2)}, u32[]{:S(2)}) async-start(bf16[32,10,2048]{2,1,0:T(8,128)(2,1)} %reshape.66), calls=%async_computation.2 | async-start | bytes 4194304 | tf_op jit(solution)/shard_map/all_to_all | solution.py:95
  398.4 11.0 %convert_bitcast_fusion = bf16[1,1024,2048]{2,1,0:T(8,128)(2,1)} fusion(bf16[1280,2048]{1,0:T(8,128)(2,1)} %reshape.69, f32[1280,1024]{1,0:T(8,128)} %copy-done.6), kind=kOutput, calls=%fused_computation.16 | convolution fusion | flops 5382602752 | bytes 14680064 | tf_op jit(solution)/shard_map/dot_general | solution.py:86
  409.4 17.3 %all-to-all-done.1 = bf16[32,10,2048]{2,1,0:T(8,128)(2,1)} async-done(((bf16[32,10,2048]{2,1,0:T(8,128)(2,1)}), bf16[32,10,2048]{2,1,0:T(8,128)(2,1)}, u32[]{:S(2)}, u32[]{:S(2)}) %all-to-all-start.1) | async-done | bytes 1310752 | tf_op jit(solution)/shard_map/all_to_all | solution.py:95
  426.7 2.5 reshape.67
  429.2 1.3 fusion.17
  (25 shorter events, 2.1 us)
Async XLA Ops:
  7.2 223.9 %copy-start = (bf16[1,128,2048]{2,1,0:T(8,128)(2,1)S(1)}, bf16[1,128,2048]{2,1,0:T(8,128)(2,1)}, u32[]{:S(2)}) copy-start(bf16[1,128,2048]{2,1,0:T(8,128)(2,1)} %param.13) | copy-start | bytes 1572868
  7.2 39.9 %all-gather.3.cloned.1.call-start = ((), (), s32[]{:S(2)}) async-start(), calls=%async_computation.4 | async-start | bytes 2621440 | tf_op jit(solution)/shard_map/all_gather | solution.py:23
  9.3 72.1 %all-gather.5.cloned.1.call-start = ((), (), s32[]{:S(2)}) async-start(), calls=%async_computation.5 | async-start | bytes 2621440 | tf_op jit(solution)/shard_map/all_gather | solution.py:24
  10.1 378.0 %reduce-scatter.2.cloned.1.call-start = ((), (), s32[]{:S(2)}) async-start(), calls=%async_computation.6 | async-start | bytes 6553600 | tf_op jit(solution)/shard_map/reduce_scatter | solution.py:89
  49.5 2.0 copy-start.2
  84.3 6.3 %copy-start.3 = (bf16[1,128,2048]{2,1,0:T(8,128)(2,1)S(1)}, bf16[1,128,2048]{2,1,0:T(8,128)(2,1)}, u32[]{:S(2)}) copy-start(bf16[1,128,2048]{2,1,0:T(8,128)(2,1)} %param.12) | copy-start | bytes 1572868
  84.3 6.3 %copy-start.4 = (f32[2048]{0:T(1024)S(1)}, f32[2048]{0:T(1024)}, u32[]{:S(2)}) copy-start(f32[2048]{0:T(1024)} %param.15) | copy-start | bytes 24580
  212.0 11.3 %copy-start.5 = (bf16[1,1024,2048]{2,1,0:T(8,128)(2,1)S(1)}, bf16[1,1024,2048]{2,1,0:T(8,128)(2,1)}, u32[]{:S(2)}) copy-start(bf16[1,1024,2048]{2,1,0:T(8,128)(2,1)} %param.17) | copy-start | bytes 12582916
  220.9 2.4 copy-start.6
  391.5 35.2 %all-to-all-start.1 = ((bf16[32,10,2048]{2,1,0:T(8,128)(2,1)}), bf16[32,10,2048]{2,1,0:T(8,128)(2,1)}, u32[]{:S(2)}, u32[]{:S(2)}) async-start(bf16[32,10,2048]{2,1,0:T(8,128)(2,1)} %reshape.66), calls=%async_computation.2 | async-start | bytes 4194304 | tf_op jit(solution)/shard_map/all_to_all | solution.py:95
  398.4 32.1 %copy-start.1 = (bf16[1,128,2048]{2,1,0:T(8,128)(2,1)S(1)}, bf16[1,128,2048]{2,1,0:T(8,128)(2,1)}, u32[]{:S(2)}) copy-start(bf16[1,128,2048]{2,1,0:T(8,128)(2,1)} %param.13) | copy-start | bytes 1572868
Sparse Core Ops, SparseCore 0:
  10.2 36.7 all-gather.2
  48.7 32.6 all-gather.4
  231.1 143.3 reduce-scatter.1
where the time goes:
time: 438 us; the launch traced here: 437 us
  blocking collectives  229 us (52%)
  waiting for transfers between devices  77.8 us (18%)
  matrix products  57.2 us (13%)
  local copies, waits for them, and re-layouts  48.2 us (11%)
  between operations  13.9 us (3%)
  starting transfers between devices  6.98 us (2%)
    all_to_all x1, blocking collectives, shards(): lax.all_to_all(wide_g, ('dp', 'seq', 'expert'), split_axis=0, concat_axis...  122 us
    all_to_all x1, blocking collectives, shards(): lax.all_to_all(wide_x, ('dp', 'seq', 'expert'), split_axis=0, concat_axis...  107 us
    all_gather x1, waiting for transfers between devices, shards(): key_block = lax.all_gather(keys, 'seq', axis=1, tiled=True)  31.2 us
    all_gather x1, waiting for transfers between devices, shards(): value_block = lax.all_gather(values, 'seq', axis=1, tiled=True)  28.6 us
    dot_general x1, matrix products, shards(): lax.dot_general(inputs, d_pre, (((0,), (0,)), ((), ())), preferred_elemen...  20.1 us
    all_to_all x1, waiting for transfers between devices, shards(): lax.all_to_all(summed.reshape(owners, capacity, model_width), ('seq', 'ex...  17.3 us
    dot_general x1, matrix products, shards(): lax.dot_general(hidden, grads_in, (((0,), (0,)), ((), ())), preferred_ele...  11 us
    reshape x1, local copies, waits for them, and re-layouts, shards(): grads_in = arrived_g.reshape(slot_count, model_width)  9.87 us
  transfers between devices with their start and end apart: 4, of which 3 were waited for; matrix products, arithmetic and copies ran while one was open for 13% of the time, Pallas kernels for 0%

commit v1 on v0

v1 whole, which is shorter than its diff:
```python
import math

import jax
import jax.numpy as jnp
from jax import lax
from jax.experimental import pallas as pl
from jax.experimental.pallas import tpu as pltpu
from jax.sharding import PartitionSpec as P

HEADS = 16
CAPACITY = 10
EPS = 1e-05
F32 = jnp.float32
BF16 = jnp.bfloat16
MIB = 1 << 20


def params(mib, **kw):
    return pltpu.CompilerParams(vmem_limit_bytes=mib * MIB, **kw)


def cost(flops, nbytes, trans=0):
    return pl.CostEstimate(flops=flops, bytes_accessed=nbytes, transcendentals=trans)


def struct(shape, dtype=BF16):
    return jax.ShapeDtypeStruct(shape, dtype)


def dot(a, b, ca=1, cb=0):
    return lax.dot_general(a, b, (((ca,), (cb,)), ((), ())), preferred_element_type=F32)


def shift(x, axis, step):
    n = lax.axis_size(axis)
    return lax.ppermute(x, axis, [(i, (i + step) % n) for i in range(n)])


def split_kernel(me_ref, q_ref, k_ref, v_ref, *outs):
    width = outs[0].shape[2]
    for r, out in enumerate(outs):
        at = pl.multiple_of(((me_ref[0] + r) % 4) * width, width)
        for i, ref in enumerate((q_ref, k_ref, v_ref)):
            out[i] = ref[0, :, pl.ds(at, width)]


def split_heads(me, q, k, v):
    rows, width = q.shape[1], q.shape[2] // 4
    vm = pl.BlockSpec(memory_space=pltpu.VMEM)
    return pl.pallas_call(
        split_kernel,
        out_shape=[struct((3, rows, width))] * 4,
        in_specs=[pl.BlockSpec(memory_space=pltpu.SMEM), vm, vm, vm],
        out_specs=[vm] * 4,
        compiler_params=params(12),
        cost_estimate=cost(0, 3 << 20),
        name="split_heads",
    )(me, q, k, v)


def attention_kernel(scale, dim, p0, p1, p2, p3, o0, o1, o2, o3):
    pieces, outs = (p0, p1, p2, p3), (o0, o1, o2, o3)
    rows = p0.shape[1]
    for h in range(p0.shape[2] // dim):
        cols = slice(h * dim, (h + 1) * dim)
        k = jnp.concatenate([p[1, :, cols] for p in pieces], 0)
        v = jnp.concatenate([p[2, :, cols] for p in pieces], 0)
        q = jnp.concatenate([p[0, :, cols] for p in pieces], 0)
        scores = dot(q, k, 1, 1) * scale
        weights = jnp.exp(scores - jnp.max(scores, axis=-1, keepdims=True))
        totals = jnp.sum(weights, axis=-1, keepdims=True)
        res = dot(weights.astype(BF16), v) / totals
        for i, o in enumerate(outs):
            o[:, cols] = res[i * rows : (i + 1) * rows].astype(BF16)


def attention(pieces, dim):
    _, rows, width = pieces[0].shape
    vm = pl.BlockSpec(memory_space=pltpu.VMEM)
    scale = 1.0 / math.sqrt(dim)
    return pl.pallas_call(
        lambda *refs: attention_kernel(scale, dim, *refs),
        out_shape=[struct((rows, width))] * 4,
        in_specs=[vm] * 4,
        out_specs=[vm] * 4,
        compiler_params=params(28),
        cost_estimate=cost(16 * rows * rows * width * 4, 2 << 20, 1 << 20),
        name="attention",
    )(*pieces)


def place_rows(send_ref, tgt, parts):
    tokens = tgt.shape[1]
    chunk = 320
    for c in range(send_ref.shape[0] // chunk):
        row = lax.broadcasted_iota(jnp.int32, (chunk, tokens), 0) + c * chunk
        acc = None
        for q, part in enumerate(parts):
            hot = jnp.where(row == tgt + q * CAPACITY, 1.0, 0.0).astype(BF16)
            term = dot(hot, part)
            acc = term if acc is None else acc + term
        send_ref[c * chunk : (c + 1) * chunk, :] = acc.astype(BF16)


def route_kernel(owners, zone_ref, g_ref, tgt_ref, send_ref):
    zone = zone_ref[...]
    tokens = zone.shape[1]
    hot = jnp.where(lax.broadcasted_iota(jnp.int32, (owners, tokens), 0) == zone, 1.0, 0.0)
    upper = jnp.where(
        lax.broadcasted_iota(jnp.int32, (tokens, tokens), 0)
        <= lax.broadcasted_iota(jnp.int32, (tokens, tokens), 1),
        1.0,
        0.0,
    )
    rank = dot(hot.astype(BF16), upper.astype(BF16))
    slot = jnp.sum(hot * rank, axis=0, keepdims=True) - 1.0
    tgt = zone * (4 * CAPACITY) + slot.astype(jnp.int32)
    tgt_ref[...] = tgt
    width = send_ref.shape[1]
    place_rows(send_ref, tgt, [g_ref[0, :, q * width : (q + 1) * width] for q in range(4)])


def route(zone_row, cot, owners):
    tokens, model = cot.shape[1], cot.shape[2]
    vm = pl.BlockSpec(memory_space=pltpu.VMEM)
    return pl.pallas_call(
        lambda *refs: route_kernel(owners, *refs),
        out_shape=[struct((1, tokens), jnp.int32), struct((owners * 4 * CAPACITY, model // 4))],
        in_specs=[vm] * 2,
        out_specs=[vm] * 2,
        compiler_params=params(16),
        cost_estimate=cost(700_000_000, 2 << 20),
        name="route",
    )(zone_row, cot)


def norm_kernel(me_ref, a0, a1, a2, a3, resid_ref, gain_ref, tgt_ref, mixed_ref, send_ref):
    width = a0.shape[1]
    for r, a in enumerate((a0, a1, a2, a3)):
        cols = pl.ds(pl.multiple_of(((me_ref[0] + r) % 4) * width, width), width)
        mixed_ref[:, cols] = resid_ref[0, :, cols].astype(F32) + a[...].astype(F32)
    mixed = mixed_ref[...]
    inv = lax.rsqrt(jnp.mean(mixed * mixed, axis=-1, keepdims=True) + EPS)
    normed = (mixed * inv * gain_ref[...]).astype(BF16)
    place_rows(send_ref, tgt_ref[...], [normed[:, q * width : (q + 1) * width] for q in range(4)])


def norm(me, att, resid, gain, tgt, owners):
    tokens, model = resid.shape[1], resid.shape[2]
    vm = pl.BlockSpec(memory_space=pltpu.VMEM)
    return pl.pallas_call(
        norm_kernel,
        out_shape=[struct((tokens, model), F32), struct((owners * 4 * CAPACITY, model // 4))],
        in_specs=[pl.BlockSpec(memory_space=pltpu.SMEM)] + [vm] * 7,
        out_specs=[vm] * 2,
        compiler_params=params(20),
        cost_estimate=cost(700_000_000, 4 << 20),
        name="norm",
    )(me, *att, resid, gain, tgt)


def regroup(size):
    per = size // 4
    row = lax.broadcasted_iota(jnp.int32, (size, size), 0)
    col = lax.broadcasted_iota(jnp.int32, (size, size), 1)
    quarter, rest = row // per, row % per
    want = (rest // CAPACITY) * (4 * CAPACITY) + quarter * CAPACITY + rest % CAPACITY
    return jnp.where(col == want, 1.0, 0.0).astype(BF16)


def unpack_kernel(hot_ref, got_ref, *outs):
    size = hot_ref.shape[0]
    per, width = size // 4, got_ref.shape[1]
    groups = got_ref.shape[0] // size
    each = groups // len(outs)
    for g in range(groups):
        rows = dot(hot_ref[...], got_ref[g * size : (g + 1) * size, :]).astype(BF16)
        at = (g % each) * per
        for q in range(4):
            outs[g // each][at : at + per, q * width : (q + 1) * width] = rows[
                q * per : (q + 1) * per
            ]


def unpack(hot, got, halves):
    rows, width = got.shape
    vm = pl.BlockSpec(memory_space=pltpu.VMEM)
    return pl.pallas_call(
        unpack_kernel,
        out_shape=[struct((rows // 4 // halves, width * 4))] * halves,
        in_specs=[vm] * 2,
        out_specs=[vm] * halves,
        compiler_params=params(14),
        cost_estimate=cost(420_000_000, 3 << 20),
        name="unpack",
    )(hot, got)


def pack_kernel(hot_ref, oa, ob, fa, fb, ga, gb, send_ref):
    size = hot_ref.shape[0]
    per, width = size // 4, send_ref.shape[1]
    groups = send_ref.shape[0] // size
    each = groups // 2
    for g in range(groups):
        trio = (oa, fa, ga) if g < each else (ob, fb, gb)
        at = slice((g % each) * per, (g % each) * per + per)
        total = sum(t[at, :].astype(F32) for t in trio[1:]) + trio[0][at, :].astype(F32)
        total = total.astype(BF16)
        stack = jnp.concatenate([total[:, q * width : (q + 1) * width] for q in range(4)], 0)
        send_ref[g * size : (g + 1) * size, :] = dot(hot_ref[...], stack, 0, 0).astype(BF16)


def pack(hot, six):
    rows, model = six[0].shape
    vm = pl.BlockSpec(memory_space=pltpu.VMEM)
    return pl.pallas_call(
        pack_kernel,
        out_shape=struct((rows * 8, model // 4)),
        in_specs=[vm] * 7,
        out_specs=vm,
        compiler_params=params(20),
        cost_estimate=cost(420_000_000, 6 << 20),
        name="pack",
    )(hot, *six)


def final_kernel(tgt_ref, mixed_ref, got_ref, out_ref):
    tgt = tgt_ref[...]
    tokens, width = tgt.shape[1], got_ref.shape[1]
    row = lax.broadcasted_iota(jnp.int32, (got_ref.shape[0], tokens), 0)
    got = got_ref[...]
    for q in range(4):
        hot = jnp.where(row == tgt + q * CAPACITY, 1.0, 0.0).astype(BF16)
        cols = slice(q * width, (q + 1) * width)
        out_ref[0, :, cols] = (mixed_ref[:, cols] + dot(hot, got, 0, 0)).astype(BF16)


def final(tgt, mixed, got):
    vm = pl.BlockSpec(memory_space=pltpu.VMEM)
    return pl.pallas_call(
        final_kernel,
        out_shape=struct((1,) + mixed.shape),
        in_specs=[vm] * 3,
        out_specs=vm,
        compiler_params=params(16),
        cost_estimate=cost(700_000_000, 3 << 20),
        name="combine",
    )(tgt, mixed, got)


def expert_kernel(plane_ref, xa, xb, g_ref, win, wout, hid_ref, dpre_ref, oa, ob, x_all, acc):
    step = pl.program_id(0)
    half = xa.shape[0]

    @pl.when(step == 0)
    def _():
        x_all[:half] = xa[...]
        x_all[half:] = xb[...]

    pre = dot(x_all[...], win[0])
    act, pull = jax.vjp(jax.nn.gelu, pre)
    hidden = act.astype(BF16)
    hid_ref[...] = hidden
    back = dot(g_ref[...], wout[0], 1, 1)
    dpre_ref[...] = pull(back)[0].astype(BF16)
    term = dot(hidden, wout[0])

    @pl.when(step == 0)
    def _():
        acc[...] = term

    @pl.when(step > 0)
    def _():
        acc[...] += term

    @pl.when(step == pl.num_programs(0) - 1)
    def _():
        oa[...] = acc[:half].astype(BF16)
        ob[...] = acc[half:].astype(BF16)


def expert(plane, xa, xb, g_all, w_in, w_out):
    half, model = xa.shape
    rows, hidden = 2 * half, w_in.shape[2]
    block = 256
    whole = pl.BlockSpec((half, model), lambda j, p: (0, 0))
    part = pl.BlockSpec((rows, block), lambda j, p: (0, j))
    return pl.pallas_call(
        expert_kernel,
        grid_spec=pltpu.PrefetchScalarGridSpec(
            num_scalar_prefetch=1,
            grid=(hidden // block,),
            in_specs=[
                whole,
                whole,
                pl.BlockSpec((rows, model), lambda j, p: (p[0], 0)),
                pl.BlockSpec((1, model, block), lambda j, p: (0, 0, j)),
                pl.BlockSpec((1, block, model), lambda j, p: (0, j, 0)),
            ],
            out_specs=[part, part, whole, whole],
            scratch_shapes=[pltpu.VMEM((rows, model), BF16), pltpu.VMEM((rows, model), F32)],
        ),
        out_shape=[struct((rows, hidden))] * 2 + [struct((half, model))] * 2,
        compiler_params=params(32),
        cost_estimate=cost(6 * rows * model * hidden, 12 << 20, rows * hidden),
        name="expert",
    )(plane, xa, xb, g_all, w_in, w_out)


def grad_kernel(planes, *refs):
    xs, ds, hs, gs = refs[:8], refs[8:12], refs[12:16], refs[16:20]
    first, second, x_all, d_all, h_all, g_all = refs[20:]
    step = pl.program_id(0)
    rows = ds[0].shape[0]

    @pl.when(step == 0)
    def _():
        for i in range(4):
            d_all[i * rows : (i + 1) * rows] = ds[i][...]
            g_all[i * rows : (i + 1) * rows] = gs[i][...]

    half = rows // 2
    for i in range(8):
        x_all[i * half : (i + 1) * half] = xs[i][...]
    for i in range(4):
        h_all[i * rows : (i + 1) * rows] = hs[i][...]
    first[0] = dot(x_all[...], d_all[...], 0, 0).astype(BF16)
    second[0] = dot(h_all[...], g_all[...], 0, 0).astype(BF16)


def grads(planes, xs, ds, hs, g_all):
    half, model = xs[0].shape
    rows, hidden = ds[0].shape
    steps = 8
    xb, hb = model // steps, hidden // steps
    whole = lambda r, c: pl.BlockSpec((r, c), lambda j, p: (0, 0))

    def g_spec(i):
        return pl.BlockSpec((rows, model), lambda j, p: (p[i], 0))

    return pl.pallas_call(
        grad_kernel,
        grid_spec=pltpu.PrefetchScalarGridSpec(
            num_scalar_prefetch=1,
            grid=(steps,),
            in_specs=[pl.BlockSpec((half, xb), lambda j, p: (0, j))] * 8
            + [whole(rows, hidden)] * 4
            + [pl.BlockSpec((rows, hb), lambda j, p: (0, j))] * 4
            + [g_spec(i) for i in range(4)],
            out_specs=[
                pl.BlockSpec((1, xb, hidden), lambda j, p: (0, j, 0)),
                pl.BlockSpec((1, hb, model), lambda j, p: (0, j, 0)),
            ],
            scratch_shapes=[
                pltpu.VMEM((4 * rows, xb), BF16),
                pltpu.VMEM((4 * rows, hidden), BF16),
                pltpu.VMEM((4 * rows, hb), BF16),
                pltpu.VMEM((4 * rows, model), BF16),
            ],
        ),
        out_shape=[struct((1, model, hidden)), struct((1, hidden, model))],
        compiler_params=params(44),
        cost_estimate=cost(16 * rows * model * hidden, 24 << 20),
        name="grads",
    )(planes, *xs, *ds, *hs, *([g_all] * 4))


def shards(queries, keys, values, resid, cotangent, zone_ids, norm_gain, w_in, w_out):
    model = queries.shape[2]
    owners = lax.axis_size("seq") * lax.axis_size("expert")
    seq_at = lax.axis_index("seq").astype(jnp.int32).reshape(1)
    dp_at = lax.axis_index("dp").astype(jnp.int32)
    planes = [((dp_at + r) % 4).reshape(1) for r in (0, 3, 1, 2)]

    def exchange(blocks):
        shaped = blocks.reshape(owners, 4 * CAPACITY, model // 4)
        got = lax.all_to_all(shaped, ("seq", "expert"), 0, 0, tiled=True)
        return got.reshape(owners * 4 * CAPACITY, model // 4)

    hot = regroup(8 * 4 * CAPACITY)
    sent = split_heads(seq_at, queries, keys, values)
    pieces = [sent[0]] + [shift(sent[r], "seq", r) for r in (1, 2, 3)]
    tgt, send_g = route(zone_ids[:, :, 0], cotangent, owners)
    (own_g,) = unpack(hot, exchange(send_g), 1)
    g_all = lax.all_gather(own_g, "dp", axis=0, tiled=True)

    att = attention(pieces, model // HEADS)
    att = [att[0]] + [shift(att[r], "seq", -r) for r in (1, 2, 3)]
    mixed, send_x = norm(seq_at, att, resid, norm_gain.reshape(1, model), tgt, owners)
    oxa, oxb = unpack(hot, exchange(send_x), 2)
    fxa, gxb = shift(oxa, "dp", 1), shift(oxb, "dp", -1)
    fxb, gxa = shift(oxb, "dp", 1), shift(oxa, "dp", -1)
    hxa, hxb = shift(fxa, "dp", 1), shift(gxb, "dp", -1)

    pairs = [(oxa, oxb), (fxa, fxb), (gxa, gxb), (hxa, hxb)]
    done = [expert(p, a, b, g_all, w_in, w_out) for p, (a, b) in zip(planes, pairs)]
    (own_a, own_b), (prev_a, prev_b), (next_a, next_b), (far_a, far_b) = [d[2:] for d in done]
    to_next_b = shift(next_b, "dp", 1)
    to_prev_a = shift(prev_a, "dp", -1)
    via_a = shift(far_a, "dp", 1)
    via_b = shift(far_b, "dp", -1)
    next_a = (next_a.astype(F32) + via_a.astype(F32)).astype(BF16)
    prev_b = (prev_b.astype(F32) + via_b.astype(F32)).astype(BF16)
    to_next_a = shift(next_a, "dp", 1)
    to_prev_b = shift(prev_b, "dp", -1)
    grad_first, grad_second = grads(
        jnp.concatenate(planes),
        [x for pair in pairs for x in pair],
        [d[1] for d in done],
        [d[0] for d in done],
        g_all,
    )
    back = pack(hot, [own_a, own_b, to_next_a, to_next_b, to_prev_a, to_prev_b])
    layer_out = final(tgt, mixed, exchange(back))
    return (layer_out, grad_first, grad_second)


def solution(mesh):
    token = P(("dp", "expert"), "seq", None)
    first = P(("seq", "expert"), None, "dp")
    second = P(("seq", "expert"), "dp", None)
    return jax.shard_map(
        shards,
        mesh=mesh,
        in_specs=(token,) * 6 + (P(), first, second),
        out_specs=(token, first, second),
        check_vma=False,
    )
```

time: 438 us -> 260 us (0.59)
  blocking collectives: 229 us -> 23.7 us
  Pallas kernels: 0 us -> 67.4 us
  matrix products: 57.2 us -> 0 us
  starting transfers between devices: 6.98 us -> 38.8 us
  local copies, waits for them, and re-layouts: 48.2 us -> 29.8 us
  waiting for transfers between devices: 77.8 us -> 82.7 us
    all_to_all x2 -> x1, blocking collectives: 229 us -> 23.7 us  [exchange(): got = lax.all_to_all(shaped, ('seq', 'expert'), 0, 0, tiled=True)]
    pallas_call x0 -> x13, Pallas kernels: none -> 67.4 us  [the longest x4 34.6 us: expert(): pl.pallas_call(expert_kernel, grid_spec=pltpu.PrefetchScalarGridSpec(num_...]
    ppermute x0 -> x18, waiting for transfers between devices: none -> 63.5 us  [shift(): return lax.ppermute(x, axis, [(i, (i + step) % n) for i in range(n)])]
    all_gather x2 -> x1, waiting for transfers between devices: 59.8 us -> 0.01 us  [shards(): g_all = lax.all_gather(own_g, 'dp', axis=0, tiled=True)]
    dot_general x9 -> x0, matrix products: 57.2 us -> none  [the longest x1 20.1 us: shards(): lax.dot_general(inputs, d_pre, (((0,), (0,)), ((), ())), preferred_elemen...]
    reshape x5 -> x0, local copies, waits for them, and re-layouts: 27.1 us -> none  [the longest x1 9.87 us: shards(): grads_in = arrived_g.reshape(slot_count, model_width)]
    unnamed x16 -> x64, local copies, waits for them, and re-layouts: 7.63 us -> 29.8 us
    ppermute x0 -> x18, starting transfers between devices: none -> 21.2 us  [shift(): return lax.ppermute(x, axis, [(i, (i + step) % n) for i in range(n)])]
  transfers between devices with their start and end apart: 4 -> 21, of which waited for: 3 -> 10; matrix products, arithmetic and copies ran while one was open for 13% -> 1% of each run, Pallas kernels for 0% -> 22%
where the time goes in v1:
time: 260 us; the launch traced here: 259 us
  waiting for transfers between devices  82.7 us (32%)
  Pallas kernels  67.4 us (26%)
  starting transfers between devices  38.8 us (15%)
  local copies, waits for them, and re-layouts  29.8 us (11%)
  blocking collectives  23.7 us (9%)
  between operations  14.3 us (6%)
  other arithmetic  2.72 us (1%)
    ppermute x18, waiting for transfers between devices, shift(): return lax.ppermute(x, axis, [(i, (i + step) % n) for i in range(n)])  63.5 us
    pallas_call x4, Pallas kernels, expert(): pl.pallas_call(expert_kernel, grid_spec=pltpu.PrefetchScalarGridSpec(num_...  34.6 us
    unnamed x64, local copies, waits for them, and re-layouts  29.8 us
    all_to_all x1, blocking collectives, exchange(): got = lax.all_to_all(shaped, ('seq', 'expert'), 0, 0, tiled=True)  23.7 us
    ppermute x18, starting transfers between devices, shift(): return lax.ppermute(x, axis, [(i, (i + step) % n) for i in range(n)])  21.2 us
    all_to_all x2, waiting for transfers between devices, exchange(): got = lax.all_to_all(shaped, ('seq', 'expert'), 0, 0, tiled=True)  19.2 us
    pallas_call x1, Pallas kernels, grads(): pl.pallas_call(grad_kernel, grid_spec=pltpu.PrefetchScalarGridSpec(num_sc...  18.5 us
    all_to_all x2, starting transfers between devices, exchange(): got = lax.all_to_all(shaped, ('seq', 'expert'), 0, 0, tiled=True)  17.5 us
  transfers between devices with their start and end apart: 21, of which 10 were waited for; matrix products, arithmetic and copies ran while one was open for 1% of the time, Pallas kernels for 22%

profile of v1, /device:TPU:1, one launch (start us, length us, event | category | flops | bytes accessed | tf_op | source)
XLA Modules:
  0.0 259.3 jit_solution(14473437344233712696)
XLA Ops:
  8.9 2.8 %route.1 = (s32[1,128]{1,0:T(1,128)S(1)}, bf16[1280,512]{1,0:T(8,128)(2,1)}) custom-call(s32[1,128]{1,0:T(1,128)S(1)} %bitcast.18, bf16[1,128,2048]{2,1,0:T(8,128)(2,1)S(1)} %copy-done.28), custom_call_target="tpu_custom_call" | custom-call | flops 700000000 | bytes 2097152 | tf_op jit(solution)/shard_map/route/pallas_call | solution.py:126
  11.6 9.4 %all-to-all-start.1 = ((bf16[32,40,512]{2,1,0:T(8,128)(2,1)}), bf16[32,40,512]{2,1,0:T(8,128)(2,1)S(1)}, u32[]{:S(2)}, u32[]{:S(2)}) async-start(bf16[32,40,512]{2,1,0:T(8,128)(2,1)} %bitcast.6), calls=%async_computation.1 | async-start | bytes 2621440 | tf_op jit(solution)/shard_map/all_to_all | solution.py:377
  21.7 19.2 %all-to-all-done.1 = bf16[32,40,512]{2,1,0:T(8,128)(2,1)S(1)} async-done(((bf16[32,40,512]{2,1,0:T(8,128)(2,1)}), bf16[32,40,512]{2,1,0:T(8,128)(2,1)S(1)}, u32[]{:S(2)}, u32[]{:S(2)}) %all-to-all-start.1) | async-done | bytes 1310752 | tf_op jit(solution)/shard_map/all_to_all | solution.py:377
  40.8 1.9 unpack.3
  44.2 1.8 collective-permute-start.1
  47.3 9.6 %collective-permute-done.refs_1_ = bf16[3,128,512]{2,1,0:T(8,128)(2,1)S(1)} collective-permute-done((bf16[3,128,512]{2,1,0:T(8,128)(2,1)S(1)}, bf16[3,128,512]{2,1,0:T(8,128)(2,1)S(1)}, u32[]{:S(2)}, u32[]{:S(2)}) %collective-permute-start) | collective-permute-done | bytes 393248 | tf_op jit(solution)/shard_map/ppermute | solution.py:36
  56.9 6.1 %collective-permute-done.1.refs_2_ = bf16[3,128,512]{2,1,0:T(8,128)(2,1)S(1)} collective-permute-done((bf16[3,128,512]{2,1,0:T(8,128)(2,1)S(1)}, bf16[3,128,512]{2,1,0:T(8,128)(2,1)S(1)}, u32[]{:S(2)}, u32[]{:S(2)}) %collective-permute-start.1) | collective-permute-done | bytes 393248 | tf_op jit(solution)/shard_map/ppermute | solution.py:36
  64.5 1.7 attention.1
  66.3 3.5 %collective-permute-start.3 = (bf16[128,512]{1,0:T(8,128)(2,1)S(1)}, bf16[128,512]{1,0:T(8,128)(2,1)S(1)}, u32[]{:S(2)}, u32[]{:S(2)}) collective-permute-start(bf16[128,512]{1,0:T(8,128)(2,1)S(1)} %get-tuple-element.41), channel_id=1, source_target_pairs={{0,24},{8,0},{16,8},{24,16},{1,25},{9,1},{17,9},{25,17},{2,26},{10... | collective-permute-start | bytes 393224 | tf_op jit(solution)/shard_map/ppermute | solution.py:36
  70.4 4.7 %collective-permute-done.3.a1 = bf16[128,512]{1,0:T(8,128)(2,1)S(1)} collective-permute-done((bf16[128,512]{1,0:T(8,128)(2,1)S(1)}, bf16[128,512]{1,0:T(8,128)(2,1)S(1)}, u32[]{:S(2)}, u32[]{:S(2)}) %collective-permute-start.3) | collective-permute-done | bytes 131104 | tf_op jit(solution)/shard_map/ppermute | solution.py:36
  75.7 3.3 %collective-permute-done.5.a3 = bf16[128,512]{1,0:T(8,128)(2,1)S(1)} collective-permute-done((bf16[128,512]{1,0:T(8,128)(2,1)S(1)}, bf16[128,512]{1,0:T(8,128)(2,1)S(1)}, u32[]{:S(2)}, u32[]{:S(2)}) %collective-permute-start.5) | collective-permute-done | bytes 131104 | tf_op jit(solution)/shard_map/ppermute | solution.py:36
  79.0 1.8 norm.1
  80.7 23.7 %all_to_all.15 = bf16[32,40,512]{2,1,0:T(8,128)(2,1)S(1)} all-to-all(bf16[32,40,512]{2,1,0:T(8,128)(2,1)S(1)} %bitcast.16), channel_id=1, replica_groups=mesh['dp'=4,'seq'=4,'expert'=8] {'seq','expert'}, dimensions={0} | all-to-all | bytes 2621440 | tf_op jit(solution)/shard_map/all_to_all | solution.py:377
  108.2 14.7 %collective-permute-done.8.xa.refs_2_ = bf16[160,2048]{1,0:T(8,128)(2,1)S(1)} collective-permute-done((bf16[160,2048]{1,0:T(8,128)(2,1)S(1)}, bf16[160,2048]{1,0:T(8,128)(2,1)S(1)}, u32[]{:S(2)}, u32[]{:S(2)}) %collective-permute-start.8) | collective-permute-done | bytes 655392 | tf_op jit(solution)/shard_map/ppermute | solution.py:36
  122.8 2.7 %collective-permute-start.10 = (bf16[160,2048]{1,0:T(8,128)(2,1)}, bf16[160,2048]{1,0:T(8,128)(2,1)}, u32[]{:S(2)}, u32[]{:S(2)}) collective-permute-start(bf16[160,2048]{1,0:T(8,128)(2,1)} %collective-permute-done.7.xb.refs_5_), channel_id=1, source_target_pairs={{0,96},{32,0},{64,32},{96,64},{1,97},{33,1},{65,33},{97,65},{2,98}... | collective-permute-start | bytes 1966088 | tf_op jit(solution)/shard_map/ppermute | solution.py:36
  127.0 12.5 %collective-permute-done.9.xa.refs_6_ = bf16[160,2048]{1,0:T(8,128)(2,1)} collective-permute-done((bf16[160,2048]{1,0:T(8,128)(2,1)S(1)}, bf16[160,2048]{1,0:T(8,128)(2,1)}, u32[]{:S(2)}, u32[]{:S(2)}) %collective-permute-start.9) | collective-permute-done | bytes 655392 | tf_op jit(solution)/shard_map/ppermute | solution.py:36
  139.5 2.5 copy-done
  142.0 2.2 copy-done.2
  144.1 2.2 copy-done.4
  146.3 8.6 %expert.6 = (bf16[320,1024]{1,0:T(8,128)(2,1)S(1)}, bf16[320,1024]{1,0:T(8,128)(2,1)S(1)}, bf16[160,2048]{1,0:T(8,128)(2,1)S(1)}, bf16[160,2048]{1,0:T(8,128)(2,1)S(1)}) custom-call(s32[1]{0:T(128)} %bitcast.9.plane_ref, bf16[160,2048]{1,0:T(8,128)(2,1)} %collective-permute-done.9.xa.refs_6_, bf16[160,2048]{1,0:T(8,128)(2,1)} %collective-permute-done.10.xb.refs_7_, ...), custom_call_target="tpu_custom_call" | custom-call | flops 4026531840 | bytes 12582912 | tf_op jit(solution)/shard_map/expert/pallas_call | solution.py:288
  156.6 9.4 %expert.5 = (bf16[320,1024]{1,0:T(8,128)(2,1)S(1)}, bf16[320,1024]{1,0:T(8,128)(2,1)S(1)}, bf16[160,2048]{1,0:T(8,128)(2,1)S(1)}, bf16[160,2048]{1,0:T(8,128)(2,1)}) custom-call(s32[1]{0:T(128)} %bitcast.8.plane_ref, bf16[160,2048]{1,0:T(8,128)(2,1)} %collective-permute-done.6.xa.refs_4_, bf16[160,2048]{1,0:T(8,128)(2,1)} %collective-permute-done.7.xb.refs_5_, ...), custom_call_target="tpu_custom_call" | custom-call | flops 4026531840 | bytes 12582912 | tf_op jit(solution)/shard_map/expert/pallas_call | solution.py:288
  170.4 9.2 %expert.7 = (bf16[320,1024]{1,0:T(8,128)(2,1)S(1)}, bf16[320,1024]{1,0:T(8,128)(2,1)S(1)}, bf16[160,2048]{1,0:T(8,128)(2,1)}, bf16[160,2048]{1,0:T(8,128)(2,1)S(1)}) custom-call(s32[1]{0:T(128)} %bitcast.10.plane_ref, bf16[160,2048]{1,0:T(8,128)(2,1)S(1)} %collective-permute-done.8.xa.refs_2_, bf16[160,2048]{1,0:T(8,128)(2,1)} %collective-permute-done.14.xb.refs_3_, ...), custom_call_target="tpu_custom_call" | custom-call | flops 4026531840 | bytes 12582912 | tf_op jit(solution)/shard_map/expert/pallas_call | solution.py:288
  183.2 2.7 %collective-permute-start.17 = (bf16[160,2048]{1,0:T(8,128)(2,1)}, bf16[160,2048]{1,0:T(8,128)(2,1)}, u32[]{:S(2)}, u32[]{:S(2)}) collective-permute-start(bf16[160,2048]{1,0:T(8,128)(2,1)} %add_convert_fusion), channel_id=1, source_target_pairs={{0,96},{32,0},{64,32},{96,64},{1,97},{33,1},{65,33},{97,65},{2,98}... | collective-permute-start | bytes 1966088 | tf_op jit(solution)/shard_map/ppermute | solution.py:36
  185.8 2.5 copy-done.1
  188.3 2.2 copy-done.3
  190.5 2.2 copy-done.5
  192.7 7.4 %expert.4 = (bf16[320,1024]{1,0:T(8,128)(2,1)S(1)}, bf16[320,1024]{1,0:T(8,128)(2,1)S(1)}, bf16[160,2048]{1,0:T(8,128)(2,1)S(1)}, bf16[160,2048]{1,0:T(8,128)(2,1)S(1)}) custom-call(s32[1]{0:T(128)} %bitcast.3.plane_ref, bf16[160,2048]{1,0:T(8,128)(2,1)S(1)} %get-tuple-element.46.xa.refs_0_, bf16[160,2048]{1,0:T(8,128)(2,1)S(1)} %get-tuple-element.47.xb.refs_1_, ...), custom_call_target="tpu_custom_call" | custom-call | flops 4026531840 | bytes 12582912 | tf_op jit(solution)/shard_map/expert/pallas_call | solution.py:288
  200.2 10.6 %collective-permute-done.17.gb = bf16[160,2048]{1,0:T(8,128)(2,1)} collective-permute-done((bf16[160,2048]{1,0:T(8,128)(2,1)}, bf16[160,2048]{1,0:T(8,128)(2,1)}, u32[]{:S(2)}, u32[]{:S(2)}) %collective-permute-start.17) | collective-permute-done | bytes 655392 | tf_op jit(solution)/shard_map/ppermute | solution.py:36
  210.8 3.5 %pack.1 = bf16[1280,512]{1,0:T(8,128)(2,1)} custom-call(bf16[320,320]{1,0:T(8,128)(2,1)S(1)} %select_convert_fusion.hot_ref, bf16[160,2048]{1,0:T(8,128)(2,1)S(1)} %get-tuple-element.49.oa, bf16[160,2048]{1,0:T(8,128)(2,1)S(1)} %get-tuple-element.50.ob, bf16[160,2048]{1,0:T(8,128)(2,1)} %collective-permute-done.12.fa, ...), custom_call_target="tpu_custom_call" | custom-call | flops 420000000 | bytes 6291456 | tf_op jit(solution)/shard_map/pack/pallas_call | solution.py:216
  214.3 8.1 %all-to-all-start.2 = ((bf16[32,40,512]{2,1,0:T(8,128)(2,1)}), bf16[32,40,512]{2,1,0:T(8,128)(2,1)S(1)}, u32[]{:S(2)}, u32[]{:S(2)}) async-start(bf16[32,40,512]{2,1,0:T(8,128)(2,1)} %bitcast.11), calls=%async_computation.2 | async-start | bytes 2621440 | tf_op jit(solution)/shard_map/all_to_all | solution.py:377
  232.3 18.5 %grads.1 = (bf16[1,2048,1024]{2,1,0:T(8,128)(2,1)}, bf16[1,1024,2048]{2,1,0:T(8,128)(2,1)}) custom-call(s32[4]{0:T(128)S(1)} %pad_add_fusion.planes, bf16[160,2048]{1,0:T(8,128)(2,1)S(1)} %get-tuple-element.46.xa.refs_0_, bf16[160,2048]{1,0:T(8,128)(2,1)S(1)} %copy-done.7, bf16[160,2048]{1,0:T(8,128)(2,1)S(1)} %copy-done.9, ...), custom_call_target="tpu_custom_call" | custom-call | flops 10737418240 | bytes 25165824 | tf_op jit(solution)/shard_map/grads/pallas_call | solution.py:341
  250.7 1.7 combine.1
  (96 shorter events, 32.5 us)
Async XLA Ops:
  11.6 29.2 %all-to-all-start.1 = ((bf16[32,40,512]{2,1,0:T(8,128)(2,1)}), bf16[32,40,512]{2,1,0:T(8,128)(2,1)S(1)}, u32[]{:S(2)}, u32[]{:S(2)}) async-start(bf16[32,40,512]{2,1,0:T(8,128)(2,1)} %bitcast.6), calls=%async_computation.1 | async-start | bytes 2621440 | tf_op jit(solution)/shard_map/all_to_all | solution.py:377
  21.1 118.4 %all-gather.2.cloned.1.call-start = ((), (), s32[]{:S(2)}) async-start(), calls=%async_computation.3 | async-start | bytes 6553600 | tf_op jit(solution)/shard_map/all_gather | solution.py:385
  44.1 34.9 %copy-start.29 = (bf16[1,128,2048]{2,1,0:T(8,128)(2,1)S(1)}, bf16[1,128,2048]{2,1,0:T(8,128)(2,1)}, u32[]{:S(2)}) copy-start(bf16[1,128,2048]{2,1,0:T(8,128)(2,1)} %resid_ref.1) | copy-start | bytes 1572868
  44.1 34.9 %copy-start.30 = (f32[2048]{0:T(1024)S(1)}, f32[2048]{0:T(1024)}, u32[]{:S(2)}) copy-start(f32[2048]{0:T(1024)} %param.15) | copy-start | bytes 24580
  44.1 12.8 %collective-permute-start = (bf16[3,128,512]{2,1,0:T(8,128)(2,1)S(1)}, bf16[3,128,512]{2,1,0:T(8,128)(2,1)S(1)}, u32[]{:S(2)}, u32[]{:S(2)}) collective-permute-start(bf16[3,128,512]{2,1,0:T(8,128)(2,1)S(1)} %get-tuple-element.37), channel_id=1, source_target_pairs={{0,8},{8,16},{16,24},{24,0},{1,9},{9,17},{17,25},{25,1},{2,10},{10... | collective-permute-start | bytes 1179656 | tf_op jit(solution)/shard_map/ppermute | solution.py:36
  44.2 18.8 %collective-permute-start.1 = (bf16[3,128,512]{2,1,0:T(8,128)(2,1)S(1)}, bf16[3,128,512]{2,1,0:T(8,128)(2,1)S(1)}, u32[]{:S(2)}, u32[]{:S(2)}) collective-permute-start(bf16[3,128,512]{2,1,0:T(8,128)(2,1)S(1)} %get-tuple-element.38), channel_id=1, source_target_pairs={{0,16},{8,24},{16,0},{24,8},{1,17},{9,25},{17,1},{25,9},{2,18},{10... | collective-permute-start | bytes 1179656 | tf_op jit(solution)/shard_map/ppermute | solution.py:36
  46.0 18.5 %collective-permute-start.2 = (bf16[3,128,512]{2,1,0:T(8,128)(2,1)S(1)}, bf16[3,128,512]{2,1,0:T(8,128)(2,1)S(1)}, u32[]{:S(2)}, u32[]{:S(2)}) collective-permute-start(bf16[3,128,512]{2,1,0:T(8,128)(2,1)S(1)} %get-tuple-element.39), channel_id=1, source_target_pairs={{0,24},{8,0},{16,8},{24,16},{1,25},{9,1},{17,9},{25,17},{2,26},{10... | collective-permute-start | bytes 1179656 | tf_op jit(solution)/shard_map/ppermute | solution.py:36
  66.3 8.9 %collective-permute-start.3 = (bf16[128,512]{1,0:T(8,128)(2,1)S(1)}, bf16[128,512]{1,0:T(8,128)(2,1)S(1)}, u32[]{:S(2)}, u32[]{:S(2)}) collective-permute-start(bf16[128,512]{1,0:T(8,128)(2,1)S(1)} %get-tuple-element.41), channel_id=1, source_target_pairs={{0,24},{8,0},{16,8},{24,16},{1,25},{9,1},{17,9},{25,17},{2,26},{10... | collective-permute-start | bytes 393224 | tf_op jit(solution)/shard_map/ppermute | solution.py:36
  69.7 6.0 %collective-permute-start.4 = (bf16[128,512]{1,0:T(8,128)(2,1)S(1)}, bf16[128,512]{1,0:T(8,128)(2,1)S(1)}, u32[]{:S(2)}, u32[]{:S(2)}) collective-permute-start(bf16[128,512]{1,0:T(8,128)(2,1)S(1)} %get-tuple-element.42), channel_id=1, source_target_pairs={{0,16},{8,24},{16,0},{24,8},{1,17},{9,25},{17,1},{25,9},{2,18},{10... | collective-permute-start | bytes 393224 | tf_op jit(solution)/shard_map/ppermute | solution.py:36
  69.7 9.2 %collective-permute-start.5 = (bf16[128,512]{1,0:T(8,128)(2,1)S(1)}, bf16[128,512]{1,0:T(8,128)(2,1)S(1)}, u32[]{:S(2)}, u32[]{:S(2)}) collective-permute-start(bf16[128,512]{1,0:T(8,128)(2,1)S(1)} %get-tuple-element.43), channel_id=1, source_target_pairs={{0,8},{8,16},{16,24},{24,0},{1,9},{9,17},{17,25},{25,1},{2,10},{10... | collective-permute-start | bytes 393224 | tf_op jit(solution)/shard_map/ppermute | solution.py:36
  105.3 80.5 %copy-start.6 = (bf16[160,2048]{1,0:T(8,128)(2,1)}, bf16[160,2048]{1,0:T(8,128)(2,1)S(1)}, u32[]{:S(2)}) copy-start(bf16[160,2048]{1,0:T(8,128)(2,1)S(1)} %get-tuple-element.47.xb.refs_1_) | copy-start | bytes 1966084
  105.3 17.5 %collective-permute-start.8 = (bf16[160,2048]{1,0:T(8,128)(2,1)S(1)}, bf16[160,2048]{1,0:T(8,128)(2,1)S(1)}, u32[]{:S(2)}, u32[]{:S(2)}) collective-permute-start(bf16[160,2048]{1,0:T(8,128)(2,1)S(1)} %get-tuple-element.46.xa.refs_0_), channel_id=1, source_target_pairs={{0,32},{32,64},{64,96},{96,0},{1,33},{33,65},{65,97},{97,1},{2,34}... | collective-permute-start | bytes 1966088 | tf_op jit(solution)/shard_map/ppermute | solution.py:36
  106.5 16.3 %collective-permute-start.7 = (bf16[160,2048]{1,0:T(8,128)(2,1)S(1)}, bf16[160,2048]{1,0:T(8,128)(2,1)}, u32[]{:S(2)}, u32[]{:S(2)}) collective-permute-start(bf16[160,2048]{1,0:T(8,128)(2,1)S(1)} %get-tuple-element.47.xb.refs_1_), channel_id=1, source_target_pairs={{0,96},{32,0},{64,32},{96,64},{1,97},{33,1},{65,33},{97,65},{2,98}... | collective-permute-start | bytes 1966088 | tf_op jit(solution)/shard_map/ppermute | solution.py:36
  122.8 47.6 %copy-start.8 = (bf16[160,2048]{1,0:T(8,128)(2,1)}, bf16[160,2048]{1,0:T(8,128)(2,1)S(1)}, u32[]{:S(2)}) copy-start(bf16[160,2048]{1,0:T(8,128)(2,1)S(1)} %collective-permute-done.8.xa.refs_2_) | copy-start | bytes 1966084
  122.8 16.6 %collective-permute-start.9 = (bf16[160,2048]{1,0:T(8,128)(2,1)S(1)}, bf16[160,2048]{1,0:T(8,128)(2,1)}, u32[]{:S(2)}, u32[]{:S(2)}) collective-permute-start(bf16[160,2048]{1,0:T(8,128)(2,1)S(1)} %collective-permute-done.8.xa.refs_2_), channel_id=1, source_target_pairs={{0,32},{32,64},{64,96},{96,0},{1,33},{33,65},{65,97},{97,1},{2,34}... | collective-permute-start | bytes 1966088 | tf_op jit(solution)/shard_map/ppermute | solution.py:36
  122.8 16.6 %collective-permute-start.10 = (bf16[160,2048]{1,0:T(8,128)(2,1)}, bf16[160,2048]{1,0:T(8,128)(2,1)}, u32[]{:S(2)}, u32[]{:S(2)}) collective-permute-start(bf16[160,2048]{1,0:T(8,128)(2,1)} %collective-permute-done.7.xb.refs_5_), channel_id=1, source_target_pairs={{0,96},{32,0},{64,32},{96,64},{1,97},{33,1},{65,33},{97,65},{2,98}... | collective-permute-start | bytes 1966088 | tf_op jit(solution)/shard_map/ppermute | solution.py:36
  125.5 31.0 %collective-permute-start.6 = (bf16[160,2048]{1,0:T(8,128)(2,1)S(1)}, bf16[160,2048]{1,0:T(8,128)(2,1)}, u32[]{:S(2)}, u32[]{:S(2)}) collective-permute-start(bf16[160,2048]{1,0:T(8,128)(2,1)S(1)} %get-tuple-element.46.xa.refs_0_), channel_id=1, source_target_pairs={{0,96},{32,0},{64,32},{96,64},{1,97},{33,1},{65,33},{97,65},{2,98}... | collective-permute-start | bytes 1966088 | tf_op jit(solution)/shard_map/ppermute | solution.py:36
  125.8 44.6 %collective-permute-start.14 = (bf16[160,2048]{1,0:T(8,128)(2,1)S(1)}, bf16[160,2048]{1,0:T(8,128)(2,1)}, u32[]{:S(2)}, u32[]{:S(2)}) collective-permute-start(bf16[160,2048]{1,0:T(8,128)(2,1)S(1)} %get-tuple-element.47.xb.refs_1_), channel_id=1, source_target_pairs={{0,32},{32,64},{64,96},{96,0},{1,33},{33,65},{65,97},{97,1},{2,34}... | collective-permute-start | bytes 1966088 | tf_op jit(solution)/shard_map/ppermute | solution.py:36
  139.5 2.5 copy-start
  142.0 2.2 copy-start.2
  156.6 24.5 %collective-permute-start.11 = (bf16[160,2048]{1,0:T(8,128)(2,1)S(1)}, bf16[160,2048]{1,0:T(8,128)(2,1)S(1)}, u32[]{:S(2)}, u32[]{:S(2)}) collective-permute-start(bf16[160,2048]{1,0:T(8,128)(2,1)S(1)} %get-tuple-element.52), channel_id=1, source_target_pairs={{0,32},{32,64},{64,96},{96,0},{1,33},{33,65},{65,97},{97,1},{2,34}... | collective-permute-start | bytes 1966088 | tf_op jit(solution)/shard_map/ppermute | solution.py:36
  167.7 32.4 %collective-permute-start.13 = (bf16[160,2048]{1,0:T(8,128)(2,1)}, bf16[160,2048]{1,0:T(8,128)(2,1)}, u32[]{:S(2)}, u32[]{:S(2)}) collective-permute-start(bf16[160,2048]{1,0:T(8,128)(2,1)} %get-tuple-element.53), channel_id=1, source_target_pairs={{0,32},{32,64},{64,96},{96,0},{1,33},{33,65},{65,97},{97,1},{2,34}... | collective-permute-start | bytes 1966088 | tf_op jit(solution)/shard_map/ppermute | solution.py:36
  168.8 13.3 %collective-permute-start.16 = (bf16[160,2048]{1,0:T(8,128)(2,1)S(1)}, bf16[160,2048]{1,0:T(8,128)(2,1)S(1)}, u32[]{:S(2)}, u32[]{:S(2)}) collective-permute-start(bf16[160,2048]{1,0:T(8,128)(2,1)S(1)} %get-tuple-element.56), channel_id=1, source_target_pairs={{0,96},{32,0},{64,32},{96,64},{1,97},{33,1},{65,33},{97,65},{2,98}... | collective-permute-start | bytes 1966088 | tf_op jit(solution)/shard_map/ppermute | solution.py:36
  179.6 3.6 %copy-start.20 = (bf16[320,1024]{1,0:T(8,128)(2,1)}, bf16[320,1024]{1,0:T(8,128)(2,1)S(1)}, u32[]{:S(2)}) copy-start(bf16[320,1024]{1,0:T(8,128)(2,1)S(1)} %get-tuple-element.62.refs_13_) | copy-start | bytes 1966084
  179.6 3.6 %copy-start.22 = (bf16[320,1024]{1,0:T(8,128)(2,1)}, bf16[320,1024]{1,0:T(8,128)(2,1)S(1)}, u32[]{:S(2)}) copy-start(bf16[320,1024]{1,0:T(8,128)(2,1)S(1)} %get-tuple-element.58.refs_9_) | copy-start | bytes 1966084
  179.6 20.6 %collective-permute-start.15 = (bf16[160,2048]{1,0:T(8,128)(2,1)}, bf16[160,2048]{1,0:T(8,128)(2,1)S(1)}, u32[]{:S(2)}, u32[]{:S(2)}) collective-permute-start(bf16[160,2048]{1,0:T(8,128)(2,1)} %get-tuple-element.54), channel_id=1, source_target_pairs={{0,96},{32,0},{64,32},{96,64},{1,97},{33,1},{65,33},{97,65},{2,98}... | collective-permute-start | bytes 1966088 | tf_op jit(solution)/shard_map/ppermute | solution.py:36
  182.1 18.1 %collective-permute-start.12 = (bf16[160,2048]{1,0:T(8,128)(2,1)}, bf16[160,2048]{1,0:T(8,128)(2,1)}, u32[]{:S(2)}, u32[]{:S(2)}) collective-permute-start(bf16[160,2048]{1,0:T(8,128)(2,1)} %add_convert_fusion.1), channel_id=1, source_target_pairs={{0,32},{32,64},{64,96},{96,0},{1,33},{33,65},{65,97},{97,1},{2,34}... | collective-permute-start | bytes 1966088 | tf_op jit(solution)/shard_map/ppermute | solution.py:36
  183.2 27.6 %collective-permute-start.17 = (bf16[160,2048]{1,0:T(8,128)(2,1)}, bf16[160,2048]{1,0:T(8,128)(2,1)}, u32[]{:S(2)}, u32[]{:S(2)}) collective-permute-start(bf16[160,2048]{1,0:T(8,128)(2,1)} %add_convert_fusion), channel_id=1, source_target_pairs={{0,96},{32,0},{64,32},{96,64},{1,97},{33,1},{65,33},{97,65},{2,98}... | collective-permute-start | bytes 1966088 | tf_op jit(solution)/shard_map/ppermute | solution.py:36
  185.8 2.5 copy-start.1
  200.1 14.2 %copy-start.24 = (bf16[320,1024]{1,0:T(8,128)(2,1)}, bf16[320,1024]{1,0:T(8,128)(2,1)S(1)}, u32[]{:S(2)}) copy-start(bf16[320,1024]{1,0:T(8,128)(2,1)S(1)} %get-tuple-element.61.refs_12_) | copy-start | bytes 1966084
  200.1 14.1 %copy-start.26 = (bf16[320,1024]{1,0:T(8,128)(2,1)}, bf16[320,1024]{1,0:T(8,128)(2,1)S(1)}, u32[]{:S(2)}) copy-start(bf16[320,1024]{1,0:T(8,128)(2,1)S(1)} %get-tuple-element.57.refs_8_) | copy-start | bytes 1966084
  214.3 36.5 %all-to-all-start.2 = ((bf16[32,40,512]{2,1,0:T(8,128)(2,1)}), bf16[32,40,512]{2,1,0:T(8,128)(2,1)S(1)}, u32[]{:S(2)}, u32[]{:S(2)}) async-start(bf16[32,40,512]{2,1,0:T(8,128)(2,1)} %bitcast.11), calls=%async_computation.2 | async-start | bytes 2621440 | tf_op jit(solution)/shard_map/all_to_all | solution.py:377
  (21 other events, 25.6 us)
Sparse Core Ops, SparseCore 0:
  42.9 54.6 all-gather.1
